TPU v7x, 128 devices: a whole 4x4x4 slice. The times are simulated.
128 devices in a mesh: chan: 8 (over x, core), stn: 16 (over y, z).
Axes of the slice: x: 4, y: 4, z: 4, core: 2. Of those that a mesh axis runs over, the one named last changes fastest.
Arguments:
- voltages: bfloat16 [2, 1024, 535552], P(None, ('stn', 'chan')), may hold values from -6 to 6
- fir_taps: float32 [12, 1024], replicated, may hold values from -1.75 to 1.75
- band_start: int32 [8], replicated, may hold values from 0 to 1008, as said below
- band_count: int32 [8], replicated, may hold values from 1 to 16, as said below
- subarray: int32 [512], replicated, may hold values from 0 to 3
Outputs:
- visibilities: float32 [1024, 2, 128, 1024], P('stn', None, 'chan')
Inputs may be any that keep to these rules, and one draw needn't show every extreme that they name: `band_start`: ranges of different groups may intersect; some group's range starts at channel 1024 - 16. `band_count`: one group has exactly 16 channels and another exactly 1.
All inputs are finite; a program needn't handle non-finite values.
Results may differ from a plain program's by a relative error of at most 0.0038.
Values may be sent and summed in bfloat16 or wider, within the bound.
A program may use at most 512 MiB of HBM per device.

v0:
```python
import math
import jax
import jax.numpy as jnp
from jax import lax
from jax.sharding import PartitionSpec as P

NFFT = 1024
TAPS = 12
SPECTRA = 512
CMAX = 16


def make_table(band_start, band_count):
    groups = band_start.shape[0]
    slot_ids = jnp.arange(groups * CMAX, dtype=jnp.int32)
    group_of = slot_ids // CMAX
    offset = slot_ids % CMAX
    onehot = (group_of[:, None] == jnp.arange(groups, dtype=jnp.int32)[None, :]).astype(jnp.int32)
    first_chan = jnp.sum(onehot * band_start[None, :], axis=1)
    chan_count = jnp.sum(onehot * band_count[None, :], axis=1)
    channel = first_chan + offset
    live_mask = (offset < chan_count).astype(jnp.float32)
    phase_int = jnp.arange(NFFT, dtype=jnp.int32)[None, :] * channel[:, None] % NFFT
    angles = phase_int.astype(jnp.float32) * jnp.float32(2.0 * math.pi / NFFT)
    scaling = live_mask[:, None] * jnp.float32(1.0 / math.sqrt(NFFT))
    cosine = jnp.cos(angles) * scaling
    sine_part = jnp.sin(angles) * scaling
    stacked = jnp.stack(
        [jnp.stack([cosine, sine_part], axis=1), jnp.stack([-sine_part, cosine], axis=1)], axis=1
    )
    return stacked.astype(jnp.bfloat16)


def filter_frames(volt_block, fir_taps):
    width = volt_block.shape[1]
    framed = volt_block.reshape(2, width, SPECTRA + TAPS - 1, NFFT)

    def add_tap(tap_index, summed):
        window = lax.dynamic_slice_in_dim(framed, tap_index, SPECTRA, 2)
        weights = lax.dynamic_slice_in_dim(fir_taps, tap_index, 1, 0)
        return summed + window.astype(jnp.float32) * weights

    summed = lax.fori_loop(0, TAPS, add_tap, jnp.zeros((2, width, SPECTRA, NFFT), jnp.float32))
    return summed.astype(jnp.bfloat16)


def correlate_blocks(row_data, col_data):
    rotated = jnp.stack([row_data[:, 1], -row_data[:, 0]], axis=1)
    stacked = jnp.stack([row_data, rotated], axis=0)
    return jnp.einsum("osrit,srjt->iosj", stacked, col_data, preferred_element_type=jnp.float32)


def per_device(voltages, fir_taps, band_start, band_count, subarray):
    dft_table = make_table(band_start, band_count)
    frames = filter_frames(voltages, fir_taps)
    spectra = lax.dot_general(
        dft_table, frames, (((2, 3), (0, 3)), ((), ())), preferred_element_type=jnp.float32
    ).astype(jnp.bfloat16)
    turned = lax.all_to_all(spectra, "chan", split_axis=0, concat_axis=2, tiled=True)
    stn_index = lax.axis_index("stn")
    row_block = turned.shape[2]
    correlations = correlate_blocks(turned, lax.all_gather(turned, "stn", axis=2, tiled=True))
    stations = jnp.repeat(subarray, 2)
    own_subs = lax.dynamic_slice_in_dim(stations, stn_index * row_block, row_block, 0)
    same_array = (own_subs[:, None] == stations[None, :]).astype(jnp.float32)
    return correlations * (same_array / SPECTRA)[:, None, None, :]


def solution(mesh):
    in_specs = (P(None, ("stn", "chan"), None), P(), P(), P(), P())
    out_specs = P("stn", None, "chan", None)
    return jax.shard_map(
        per_device, mesh=mesh, in_specs=in_specs, out_specs=out_specs, check_vma=False
    )
```

profile of v0, /device:TPU:1, one launch (start us, length us, event | category | flops | bytes accessed | tf_op | source)
XLA Modules:
  0.0 787.5 jit_solution(7977719925354439112)
XLA Ops:
  6.5 0.0 all-gather.2.cloned.1.call-start
  6.5 0.8 select_reduce_fusion.1
  7.3 0.5 compare_select_fusion.1
  7.8 0.5 fusion.23
  8.3 0.0 copy-start.2
  8.3 0.0 copy-start.3
  8.3 493.4 %while.14 = (s32[]{:T(128)}, f32[2,8,512,1024]{3,2,1,0:T(8,128)}, bf16[2,8,523,1024]{3,1,2,0:T(8,128)(2,1)}, f32[12,1024]{1,0:T(8,128)}, s32[]{:T(128)}, /*index=5*/s32[]{:T(128)}) while((s32[]{:T(128)}, f32[2,8,512,1024]{3,2,1,0:T(8,128)}, bf16[2,8,523,1024]{3,1,2,0:T(8,128)(2,1)}, f32[12,1024]{1,0:T(8,128)}, s32[]{:T(128)}, ...), condition=%wide.region_3.4_spmd.clone, body=%wide.region_2.3_spmd.clone.sunk | while | flops 33554432 | bytes 117452888 | solution.py:43
  8.3 13.8 %constant_dynamic-slice_fusion.4 = bf16[2,8,512,1024]{3,1,2,0:T(8,128)(2,1)} fusion(bf16[2,8,523,1024]{3,1,2,0:T(8,128)(2,1)} %get-tuple-element.170, s32[]{:T(128)} %get-tuple-element.162), kind=kLoop, calls=%fused_computation.2.clone.1 | loop fusion | bytes 33554436 | tf_op jit(solution)/shard_map/while/body/eval_jaxpr/dynamic_slice | solution.py:39
  22.2 0.8 constant_dynamic-slice_fusion.5
  22.9 19.2 %select_add_fusion.2 = f32[2,8,512,1024]{3,2,1,0:T(8,128)} fusion(f32[2,8,512,1024]{3,2,1,0:T(8,128)} %get-tuple-element.163, bf16[2,8,512,1024]{3,1,2,0:T(8,128)(2,1)} %constant_dynamic-slice_fusion.4, f32[1024]{0:T(1024)S(1)} %bitcast.49, pred[]{:T(512)S(6)} %compare.21), kind=kLoop, calls=%fused_computation.clone.1 | loop fusion | flops 33554432 | bytes 83890176 | tf_op jit(solution)/shard_map/while/body/eval_jaxpr/add | solution.py:41
  42.1 13.8 %constant_dynamic-slice_fusion.4 = bf16[2,8,512,1024]{3,1,2,0:T(8,128)(2,1)} fusion(bf16[2,8,523,1024]{3,1,2,0:T(8,128)(2,1)} %get-tuple-element.170, s32[]{:T(128)} %get-tuple-element.162), kind=kLoop, calls=%fused_computation.2.clone.1 | loop fusion | bytes 33554436 | tf_op jit(solution)/shard_map/while/body/eval_jaxpr/dynamic_slice | solution.py:39
  56.0 0.8 constant_dynamic-slice_fusion.5
  56.7 27.2 %select_add_fusion.2 = f32[2,8,512,1024]{3,2,1,0:T(8,128)} fusion(f32[2,8,512,1024]{3,2,1,0:T(8,128)} %get-tuple-element.163, bf16[2,8,512,1024]{3,1,2,0:T(8,128)(2,1)} %constant_dynamic-slice_fusion.4, f32[1024]{0:T(1024)S(1)} %bitcast.49, pred[]{:T(512)S(6)} %compare.21), kind=kLoop, calls=%fused_computation.clone.1 | loop fusion | flops 33554432 | bytes 83890176 | tf_op jit(solution)/shard_map/while/body/eval_jaxpr/add | solution.py:41
  83.9 13.8 %constant_dynamic-slice_fusion.4 = bf16[2,8,512,1024]{3,1,2,0:T(8,128)(2,1)} fusion(bf16[2,8,523,1024]{3,1,2,0:T(8,128)(2,1)} %get-tuple-element.170, s32[]{:T(128)} %get-tuple-element.162), kind=kLoop, calls=%fused_computation.2.clone.1 | loop fusion | bytes 33554436 | tf_op jit(solution)/shard_map/while/body/eval_jaxpr/dynamic_slice | solution.py:39
  97.7 0.8 constant_dynamic-slice_fusion.5
  98.5 27.2 %select_add_fusion.2 = f32[2,8,512,1024]{3,2,1,0:T(8,128)} fusion(f32[2,8,512,1024]{3,2,1,0:T(8,128)} %get-tuple-element.163, bf16[2,8,512,1024]{3,1,2,0:T(8,128)(2,1)} %constant_dynamic-slice_fusion.4, f32[1024]{0:T(1024)S(1)} %bitcast.49, pred[]{:T(512)S(6)} %compare.21), kind=kLoop, calls=%fused_computation.clone.1 | loop fusion | flops 33554432 | bytes 83890176 | tf_op jit(solution)/shard_map/while/body/eval_jaxpr/add | solution.py:41
  125.7 13.8 %constant_dynamic-slice_fusion.4 = bf16[2,8,512,1024]{3,1,2,0:T(8,128)(2,1)} fusion(bf16[2,8,523,1024]{3,1,2,0:T(8,128)(2,1)} %get-tuple-element.170, s32[]{:T(128)} %get-tuple-element.162), kind=kLoop, calls=%fused_computation.2.clone.1 | loop fusion | bytes 33554436 | tf_op jit(solution)/shard_map/while/body/eval_jaxpr/dynamic_slice | solution.py:39
  139.5 0.8 constant_dynamic-slice_fusion.5
  140.3 27.2 %select_add_fusion.2 = f32[2,8,512,1024]{3,2,1,0:T(8,128)} fusion(f32[2,8,512,1024]{3,2,1,0:T(8,128)} %get-tuple-element.163, bf16[2,8,512,1024]{3,1,2,0:T(8,128)(2,1)} %constant_dynamic-slice_fusion.4, f32[1024]{0:T(1024)S(1)} %bitcast.49, pred[]{:T(512)S(6)} %compare.21), kind=kLoop, calls=%fused_computation.clone.1 | loop fusion | flops 33554432 | bytes 83890176 | tf_op jit(solution)/shard_map/while/body/eval_jaxpr/add | solution.py:41
  167.5 13.8 %constant_dynamic-slice_fusion.4 = bf16[2,8,512,1024]{3,1,2,0:T(8,128)(2,1)} fusion(bf16[2,8,523,1024]{3,1,2,0:T(8,128)(2,1)} %get-tuple-element.170, s32[]{:T(128)} %get-tuple-element.162), kind=kLoop, calls=%fused_computation.2.clone.1 | loop fusion | bytes 33554436 | tf_op jit(solution)/shard_map/while/body/eval_jaxpr/dynamic_slice | solution.py:39
  181.3 0.8 constant_dynamic-slice_fusion.5
  182.1 27.2 %select_add_fusion.2 = f32[2,8,512,1024]{3,2,1,0:T(8,128)} fusion(f32[2,8,512,1024]{3,2,1,0:T(8,128)} %get-tuple-element.163, bf16[2,8,512,1024]{3,1,2,0:T(8,128)(2,1)} %constant_dynamic-slice_fusion.4, f32[1024]{0:T(1024)S(1)} %bitcast.49, pred[]{:T(512)S(6)} %compare.21), kind=kLoop, calls=%fused_computation.clone.1 | loop fusion | flops 33554432 | bytes 83890176 | tf_op jit(solution)/shard_map/while/body/eval_jaxpr/add | solution.py:41
  209.3 13.8 %constant_dynamic-slice_fusion.4 = bf16[2,8,512,1024]{3,1,2,0:T(8,128)(2,1)} fusion(bf16[2,8,523,1024]{3,1,2,0:T(8,128)(2,1)} %get-tuple-element.170, s32[]{:T(128)} %get-tuple-element.162), kind=kLoop, calls=%fused_computation.2.clone.1 | loop fusion | bytes 33554436 | tf_op jit(solution)/shard_map/while/body/eval_jaxpr/dynamic_slice | solution.py:39
  223.1 0.8 constant_dynamic-slice_fusion.5
  223.8 27.2 %select_add_fusion.2 = f32[2,8,512,1024]{3,2,1,0:T(8,128)} fusion(f32[2,8,512,1024]{3,2,1,0:T(8,128)} %get-tuple-element.163, bf16[2,8,512,1024]{3,1,2,0:T(8,128)(2,1)} %constant_dynamic-slice_fusion.4, f32[1024]{0:T(1024)S(1)} %bitcast.49, pred[]{:T(512)S(6)} %compare.21), kind=kLoop, calls=%fused_computation.clone.1 | loop fusion | flops 33554432 | bytes 83890176 | tf_op jit(solution)/shard_map/while/body/eval_jaxpr/add | solution.py:41
  251.0 13.8 %constant_dynamic-slice_fusion.4 = bf16[2,8,512,1024]{3,1,2,0:T(8,128)(2,1)} fusion(bf16[2,8,523,1024]{3,1,2,0:T(8,128)(2,1)} %get-tuple-element.170, s32[]{:T(128)} %get-tuple-element.162), kind=kLoop, calls=%fused_computation.2.clone.1 | loop fusion | bytes 33554436 | tf_op jit(solution)/shard_map/while/body/eval_jaxpr/dynamic_slice | solution.py:39
  264.9 0.8 constant_dynamic-slice_fusion.5
  265.6 27.2 %select_add_fusion.2 = f32[2,8,512,1024]{3,2,1,0:T(8,128)} fusion(f32[2,8,512,1024]{3,2,1,0:T(8,128)} %get-tuple-element.163, bf16[2,8,512,1024]{3,1,2,0:T(8,128)(2,1)} %constant_dynamic-slice_fusion.4, f32[1024]{0:T(1024)S(1)} %bitcast.49, pred[]{:T(512)S(6)} %compare.21), kind=kLoop, calls=%fused_computation.clone.1 | loop fusion | flops 33554432 | bytes 83890176 | tf_op jit(solution)/shard_map/while/body/eval_jaxpr/add | solution.py:41
  292.8 13.8 %constant_dynamic-slice_fusion.4 = bf16[2,8,512,1024]{3,1,2,0:T(8,128)(2,1)} fusion(bf16[2,8,523,1024]{3,1,2,0:T(8,128)(2,1)} %get-tuple-element.170, s32[]{:T(128)} %get-tuple-element.162), kind=kLoop, calls=%fused_computation.2.clone.1 | loop fusion | bytes 33554436 | tf_op jit(solution)/shard_map/while/body/eval_jaxpr/dynamic_slice | solution.py:39
  306.6 0.8 constant_dynamic-slice_fusion.5
  307.4 27.2 %select_add_fusion.2 = f32[2,8,512,1024]{3,2,1,0:T(8,128)} fusion(f32[2,8,512,1024]{3,2,1,0:T(8,128)} %get-tuple-element.163, bf16[2,8,512,1024]{3,1,2,0:T(8,128)(2,1)} %constant_dynamic-slice_fusion.4, f32[1024]{0:T(1024)S(1)} %bitcast.49, pred[]{:T(512)S(6)} %compare.21), kind=kLoop, calls=%fused_computation.clone.1 | loop fusion | flops 33554432 | bytes 83890176 | tf_op jit(solution)/shard_map/while/body/eval_jaxpr/add | solution.py:41
  334.6 13.8 %constant_dynamic-slice_fusion.4 = bf16[2,8,512,1024]{3,1,2,0:T(8,128)(2,1)} fusion(bf16[2,8,523,1024]{3,1,2,0:T(8,128)(2,1)} %get-tuple-element.170, s32[]{:T(128)} %get-tuple-element.162), kind=kLoop, calls=%fused_computation.2.clone.1 | loop fusion | bytes 33554436 | tf_op jit(solution)/shard_map/while/body/eval_jaxpr/dynamic_slice | solution.py:39
  348.4 0.8 constant_dynamic-slice_fusion.5
  349.2 27.2 %select_add_fusion.2 = f32[2,8,512,1024]{3,2,1,0:T(8,128)} fusion(f32[2,8,512,1024]{3,2,1,0:T(8,128)} %get-tuple-element.163, bf16[2,8,512,1024]{3,1,2,0:T(8,128)(2,1)} %constant_dynamic-slice_fusion.4, f32[1024]{0:T(1024)S(1)} %bitcast.49, pred[]{:T(512)S(6)} %compare.21), kind=kLoop, calls=%fused_computation.clone.1 | loop fusion | flops 33554432 | bytes 83890176 | tf_op jit(solution)/shard_map/while/body/eval_jaxpr/add | solution.py:41
  376.4 13.8 %constant_dynamic-slice_fusion.4 = bf16[2,8,512,1024]{3,1,2,0:T(8,128)(2,1)} fusion(bf16[2,8,523,1024]{3,1,2,0:T(8,128)(2,1)} %get-tuple-element.170, s32[]{:T(128)} %get-tuple-element.162), kind=kLoop, calls=%fused_computation.2.clone.1 | loop fusion | bytes 33554436 | tf_op jit(solution)/shard_map/while/body/eval_jaxpr/dynamic_slice | solution.py:39
  390.2 0.8 constant_dynamic-slice_fusion.5
  390.9 27.2 %select_add_fusion.2 = f32[2,8,512,1024]{3,2,1,0:T(8,128)} fusion(f32[2,8,512,1024]{3,2,1,0:T(8,128)} %get-tuple-element.163, bf16[2,8,512,1024]{3,1,2,0:T(8,128)(2,1)} %constant_dynamic-slice_fusion.4, f32[1024]{0:T(1024)S(1)} %bitcast.49, pred[]{:T(512)S(6)} %compare.21), kind=kLoop, calls=%fused_computation.clone.1 | loop fusion | flops 33554432 | bytes 83890176 | tf_op jit(solution)/shard_map/while/body/eval_jaxpr/add | solution.py:41
  418.1 13.8 %constant_dynamic-slice_fusion.4 = bf16[2,8,512,1024]{3,1,2,0:T(8,128)(2,1)} fusion(bf16[2,8,523,1024]{3,1,2,0:T(8,128)(2,1)} %get-tuple-element.170, s32[]{:T(128)} %get-tuple-element.162), kind=kLoop, calls=%fused_computation.2.clone.1 | loop fusion | bytes 33554436 | tf_op jit(solution)/shard_map/while/body/eval_jaxpr/dynamic_slice | solution.py:39
  432.0 0.8 constant_dynamic-slice_fusion.5
  432.7 27.2 %select_add_fusion.2 = f32[2,8,512,1024]{3,2,1,0:T(8,128)} fusion(f32[2,8,512,1024]{3,2,1,0:T(8,128)} %get-tuple-element.163, bf16[2,8,512,1024]{3,1,2,0:T(8,128)(2,1)} %constant_dynamic-slice_fusion.4, f32[1024]{0:T(1024)S(1)} %bitcast.49, pred[]{:T(512)S(6)} %compare.21), kind=kLoop, calls=%fused_computation.clone.1 | loop fusion | flops 33554432 | bytes 83890176 | tf_op jit(solution)/shard_map/while/body/eval_jaxpr/add | solution.py:41
  459.9 13.8 %constant_dynamic-slice_fusion.4 = bf16[2,8,512,1024]{3,1,2,0:T(8,128)(2,1)} fusion(bf16[2,8,523,1024]{3,1,2,0:T(8,128)(2,1)} %get-tuple-element.170, s32[]{:T(128)} %get-tuple-element.162), kind=kLoop, calls=%fused_computation.2.clone.1 | loop fusion | bytes 33554436 | tf_op jit(solution)/shard_map/while/body/eval_jaxpr/dynamic_slice | solution.py:39
  473.7 0.8 constant_dynamic-slice_fusion.5
  474.5 27.2 %select_add_fusion.2 = f32[2,8,512,1024]{3,2,1,0:T(8,128)} fusion(f32[2,8,512,1024]{3,2,1,0:T(8,128)} %get-tuple-element.163, bf16[2,8,512,1024]{3,1,2,0:T(8,128)(2,1)} %constant_dynamic-slice_fusion.4, f32[1024]{0:T(1024)S(1)} %bitcast.49, pred[]{:T(512)S(6)} %compare.21), kind=kLoop, calls=%fused_computation.clone.1 | loop fusion | flops 33554432 | bytes 83890176 | tf_op jit(solution)/shard_map/while/body/eval_jaxpr/add | solution.py:41
  501.7 0.0 copy-done.2
  501.7 0.0 copy-done.3
  501.7 2.5 fusion.22
  504.2 0.1 maximum_bitcast_fusion.3
  504.3 13.0 %bitcast_convert_fusion = bf16[128,2,8,512]{3,0,2,1:T(8,128)(2,1)S(1)} fusion(bf16[128,1,2,1024]{3,0,2,1:T(8,128)(2,1)S(1)} %get-tuple-element.127, bf16[128,1,2,1024]{3,0,2,1:T(8,128)(2,1)S(1)} %get-tuple-element.126, f32[2,8,512,1024]{3,2,1,0:T(8,128)} %get-tuple-element.84), kind=kOutput, calls=%fused_computation.12 | convolution fusion | flops 4306501632 | bytes 36700160 | tf_op jit(solution)/shard_map/dot_general | solution.py:56
  517.2 0.0 copy-start.1
  517.3 1.2 copy.22
  518.4 32.1 %all_to_all.18 = bf16[128,2,8,512]{3,2,1,0:T(8,128)(2,1)S(1)} all-to-all(bf16[128,2,8,512]{3,2,1,0:T(8,128)(2,1)S(1)} %copy.22), channel_id=1, replica_groups=mesh['chan'=8,'stn'=16] {'chan'}, dimensions={0} | all-to-all | bytes 4194304 | tf_op jit(solution)/shard_map/all_to_all | solution.py:59
  550.5 1.6 copy.39
  552.1 0.0 all-gather.2.cloned.1.call-update
  552.1 0.0 copy-done.1
  552.1 0.1 broadcast_in_dim.7
  552.3 0.2 reshape.247
  552.4 0.1 dynamic_slice.17
  552.5 0.1 compare_select_fusion
  552.6 1.8 fusion.26
  554.4 1.5 maximum_bitcast_fusion
  555.9 194.4 %all-gather.2.cloned.1.call-done = bf16[16,2,1024,512]{3,2,1,0:T(8,128)(2,1)} async-done(((bf16[16,2,64,512]{3,2,1,0:T(8,128)(2,1)}), bf16[16,2,1024,512]{3,2,1,0:T(8,128)(2,1)}) %all-gather.2.cloned.1.call-update) | async-done | bytes 33554448 | tf_op jit(solution)/shard_map/all_gather | solution.py:62
  750.3 0.0 copy-done
  750.3 18.7 %bitcast_multiply_fusion = f32[64,2,16,1024]{3,0,1,2:T(8,128)} fusion(f32[64,1024]{1,0:T(8,128)S(1)} %compare_select_fusion, bf16[1,16,2,64,512]{4,3,2,0,1:T(8,128)(2,1)} %maximum_bitcast_fusion, bf16[1,16,2,64,512]{4,3,2,0,1:T(8,128)(2,1)S(1)} %bitcast.47, bf16[16,2,1024,512]{3,2,1,0:T(8,128)(2,1)} %all-gather.2.cloned.1.call-done), kind=kOutput, calls=%fused_computation.8 | convolution fusion | flops 4305453056 | bytes 46399488 | tf_op jit(solution)/shard_map/osrit,srjt->iosj/dot_general | solution.py:50
  769.1 11.6 %copy.24 = f32[64,2,16,1024]{3,2,1,0:T(8,128)} copy(f32[64,2,16,1024]{3,0,1,2:T(8,128)} %bitcast_multiply_fusion) | data formatting | bytes 16777216 | tf_op jit(solution)/shard_map/mul | solution.py:66
  (3 shorter events, 0.0 us)
Async XLA Ops:
  6.5 743.8 %all-gather.2.cloned.1.call-start = ((), (), s32[]{:S(2)}) async-start(), calls=%async_computation.1 | async-start | bytes 35651584 | tf_op jit(solution)/shard_map/all_gather | solution.py:62
  8.3 493.4 %copy-start.2 = (f32[128]{0:T(128)S(1)}, f32[128]{0:T(128)}, u32[]{:S(2)}) copy-start(f32[128]{0:T(128)} %compare_select_fusion.1) | copy-start | bytes 1540
  8.3 493.4 %copy-start.3 = (s32[128]{0:T(128)S(1)}, s32[128]{0:T(128)}, u32[]{:S(2)}) copy-start(s32[128]{0:T(128)} %fusion.23) | copy-start | bytes 1540
  517.2 34.9 %copy-start.1 = (s32[512]{0:T(512)S(1)}, s32[512]{0:T(512)}, u32[]{:S(2)}) copy-start(s32[512]{0:T(512)} %param.11) | copy-start | bytes 6148
  552.1 198.2 %copy-start = (bf16[8,16,2,8,512]{4,3,0,2,1:T(8,128)(2,1)S(1)}, bf16[8,16,2,8,512]{4,3,0,2,1:T(8,128)(2,1)}, u32[]{:S(2)}) copy-start(bf16[8,16,2,8,512]{4,3,0,2,1:T(8,128)(2,1)} %copy.39) | copy-start | bytes 6291460
Sparse Core Ops, SparseCore 0:
  552.2 198.0 all-gather.1
where the time goes:
time: 790 us; the launch traced here: 788 us
  other arithmetic  326 us (41%)
  waiting for transfers between devices  194 us (25%)
  local copies, waits for them, and re-layouts  190 us (24%)
  blocking collectives  32.1 us (4%)
  matrix products  31.7 us (4%)
  between operations  13.5 us (2%)
    add x12, other arithmetic, add_tap(): return summed + window.astype(jnp.float32) * weights  318 us
    all_gather x1, waiting for transfers between devices, per_device(): lax.all_gather(turned, 'stn', axis=2, tiled=True)  194 us
    dynamic_slice x12, local copies, waits for them, and re-layouts, add_tap(): window = lax.dynamic_slice_in_dim(framed, tap_index, SPECTRA, 2)  166 us
    all_to_all x1, blocking collectives, per_device(): lax.all_to_all(spectra, 'chan', split_axis=0, concat_axis=2, tiled=True)  32.1 us
    dot_general x1, matrix products, correlate_blocks(): jnp.einsum('osrit,srjt->iosj', stacked, col_data, preferred_element_type=...  18.7 us
  transfers between devices with their start and end apart: 1, of which 1 were waited for; matrix products, arithmetic and copies ran while one was open for 0% of the time, Pallas kernels for 0%

commit v1 on v0

--- a/solution.py
+++ b/solution.py
@@ -59,7 +59,12 @@
     turned = lax.all_to_all(spectra, "chan", split_axis=0, concat_axis=2, tiled=True)
     stn_index = lax.axis_index("stn")
     row_block = turned.shape[2]
-    correlations = correlate_blocks(turned, lax.all_gather(turned, "stn", axis=2, tiled=True))
+    correlations = correlate_blocks(
+        turned,
+        jnp.concatenate(
+            lax.all_to_all(jnp.stack([turned] * lax.axis_size("stn")), "stn", 0, 0), axis=2
+        ),
+    )
     stations = jnp.repeat(subarray, 2)
     own_subs = lax.dynamic_slice_in_dim(stations, stn_index * row_block, row_block, 0)
     same_array = (own_subs[:, None] == stations[None, :]).astype(jnp.float32)

time: 790 us -> 1240 us (1.57)
  waiting for transfers between devices: 194 us -> 615 us
  local copies, waits for them, and re-layouts: 190 us -> 223 us
  between operations: 13.5 us -> 0.1 us
    all_to_all x0 -> x1, waiting for transfers between devices: none -> 615 us  [per_device(): lax.all_to_all(jnp.stack([turned] * lax.axis_size('stn')), 'stn', 0, 0)]
    all_gather x1 -> x0, waiting for transfers between devices: 194 us -> none  [per_device(): lax.all_gather(turned, 'stn', axis=2, tiled=True)]
    reshape x0 -> x1, local copies, waits for them, and re-layouts: none -> 22.9 us  [per_device(): jnp.concatenate(lax.all_to_all(jnp.stack([turned] * lax.axis_size('stn'))...]
where the time goes in v1:
time: 1240 us; the launch traced here: 1230 us
  waiting for transfers between devices  615 us (50%)
  other arithmetic  324 us (26%)
  local copies, waits for them, and re-layouts  223 us (18%)
  blocking collectives  32.1 us (3%)
  matrix products  31.7 us (3%)
    all_to_all x1, waiting for transfers between devices, per_device(): lax.all_to_all(jnp.stack([turned] * lax.axis_size('stn')), 'stn', 0, 0)  615 us
    add x12, other arithmetic, add_tap(): return summed + window.astype(jnp.float32) * weights  318 us
    dynamic_slice x12, local copies, waits for them, and re-layouts, add_tap(): window = lax.dynamic_slice_in_dim(framed, tap_index, SPECTRA, 2)  166 us
    all_to_all x1, blocking collectives, per_device(): lax.all_to_all(spectra, 'chan', split_axis=0, concat_axis=2, tiled=True)  32.1 us
  transfers between devices with their start and end apart: 1, of which 1 were waited for; matrix products, arithmetic and copies ran while one was open for 0% of the time, Pallas kernels for 0%

profile of v1, /device:TPU:1, one launch (start us, length us, event | category | flops | bytes accessed | tf_op | source)
XLA Modules:
  0.0 1234.3 jit_solution(871834451656398997)
XLA Ops:
  0.0 0.8 select_reduce_fusion.1
  0.8 0.5 compare_select_fusion.1
  1.3 0.5 fusion.20
  1.8 0.0 copy-start.1
  1.8 0.0 copy-start.2
  1.8 493.5 %while.14 = (s32[]{:T(128)}, f32[2,8,512,1024]{3,2,1,0:T(8,128)}, bf16[2,8,523,1024]{3,1,2,0:T(8,128)(2,1)}, f32[12,1024]{1,0:T(8,128)}, s32[]{:T(128)}, /*index=5*/s32[]{:T(128)}) while((s32[]{:T(128)}, f32[2,8,512,1024]{3,2,1,0:T(8,128)}, bf16[2,8,523,1024]{3,1,2,0:T(8,128)(2,1)}, f32[12,1024]{1,0:T(8,128)}, s32[]{:T(128)}, ...), condition=%wide.region_3.4_spmd.clone, body=%wide.region_2.3_spmd.clone.sunk | while | flops 33554432 | bytes 117452888 | solution.py:43
  1.8 13.8 %constant_dynamic-slice_fusion.4 = bf16[2,8,512,1024]{3,1,2,0:T(8,128)(2,1)} fusion(bf16[2,8,523,1024]{3,1,2,0:T(8,128)(2,1)} %get-tuple-element.170, s32[]{:T(128)} %get-tuple-element.162), kind=kLoop, calls=%fused_computation.2.clone.1 | loop fusion | bytes 33554436 | tf_op jit(solution)/shard_map/while/body/eval_jaxpr/dynamic_slice | solution.py:39
  15.6 0.8 constant_dynamic-slice_fusion.5
  16.4 19.2 %select_add_fusion.2 = f32[2,8,512,1024]{3,2,1,0:T(8,128)} fusion(f32[2,8,512,1024]{3,2,1,0:T(8,128)} %get-tuple-element.163, bf16[2,8,512,1024]{3,1,2,0:T(8,128)(2,1)} %constant_dynamic-slice_fusion.4, f32[1024]{0:T(1024)S(1)} %bitcast.50, pred[]{:T(512)S(6)} %compare.21), kind=kLoop, calls=%fused_computation.clone.1 | loop fusion | flops 33554432 | bytes 83890176 | tf_op jit(solution)/shard_map/while/body/eval_jaxpr/add | solution.py:41
  35.6 13.8 %constant_dynamic-slice_fusion.4 = bf16[2,8,512,1024]{3,1,2,0:T(8,128)(2,1)} fusion(bf16[2,8,523,1024]{3,1,2,0:T(8,128)(2,1)} %get-tuple-element.170, s32[]{:T(128)} %get-tuple-element.162), kind=kLoop, calls=%fused_computation.2.clone.1 | loop fusion | bytes 33554436 | tf_op jit(solution)/shard_map/while/body/eval_jaxpr/dynamic_slice | solution.py:39
  49.5 0.8 constant_dynamic-slice_fusion.5
  50.2 27.2 %select_add_fusion.2 = f32[2,8,512,1024]{3,2,1,0:T(8,128)} fusion(f32[2,8,512,1024]{3,2,1,0:T(8,128)} %get-tuple-element.163, bf16[2,8,512,1024]{3,1,2,0:T(8,128)(2,1)} %constant_dynamic-slice_fusion.4, f32[1024]{0:T(1024)S(1)} %bitcast.50, pred[]{:T(512)S(6)} %compare.21), kind=kLoop, calls=%fused_computation.clone.1 | loop fusion | flops 33554432 | bytes 83890176 | tf_op jit(solution)/shard_map/while/body/eval_jaxpr/add | solution.py:41
  77.4 13.8 %constant_dynamic-slice_fusion.4 = bf16[2,8,512,1024]{3,1,2,0:T(8,128)(2,1)} fusion(bf16[2,8,523,1024]{3,1,2,0:T(8,128)(2,1)} %get-tuple-element.170, s32[]{:T(128)} %get-tuple-element.162), kind=kLoop, calls=%fused_computation.2.clone.1 | loop fusion | bytes 33554436 | tf_op jit(solution)/shard_map/while/body/eval_jaxpr/dynamic_slice | solution.py:39
  91.2 0.8 constant_dynamic-slice_fusion.5
  92.0 27.2 %select_add_fusion.2 = f32[2,8,512,1024]{3,2,1,0:T(8,128)} fusion(f32[2,8,512,1024]{3,2,1,0:T(8,128)} %get-tuple-element.163, bf16[2,8,512,1024]{3,1,2,0:T(8,128)(2,1)} %constant_dynamic-slice_fusion.4, f32[1024]{0:T(1024)S(1)} %bitcast.50, pred[]{:T(512)S(6)} %compare.21), kind=kLoop, calls=%fused_computation.clone.1 | loop fusion | flops 33554432 | bytes 83890176 | tf_op jit(solution)/shard_map/while/body/eval_jaxpr/add | solution.py:41
  119.2 13.8 %constant_dynamic-slice_fusion.4 = bf16[2,8,512,1024]{3,1,2,0:T(8,128)(2,1)} fusion(bf16[2,8,523,1024]{3,1,2,0:T(8,128)(2,1)} %get-tuple-element.170, s32[]{:T(128)} %get-tuple-element.162), kind=kLoop, calls=%fused_computation.2.clone.1 | loop fusion | bytes 33554436 | tf_op jit(solution)/shard_map/while/body/eval_jaxpr/dynamic_slice | solution.py:39
  133.0 0.8 constant_dynamic-slice_fusion.5
  133.8 27.2 %select_add_fusion.2 = f32[2,8,512,1024]{3,2,1,0:T(8,128)} fusion(f32[2,8,512,1024]{3,2,1,0:T(8,128)} %get-tuple-element.163, bf16[2,8,512,1024]{3,1,2,0:T(8,128)(2,1)} %constant_dynamic-slice_fusion.4, f32[1024]{0:T(1024)S(1)} %bitcast.50, pred[]{:T(512)S(6)} %compare.21), kind=kLoop, calls=%fused_computation.clone.1 | loop fusion | flops 33554432 | bytes 83890176 | tf_op jit(solution)/shard_map/while/body/eval_jaxpr/add | solution.py:41
  161.0 13.8 %constant_dynamic-slice_fusion.4 = bf16[2,8,512,1024]{3,1,2,0:T(8,128)(2,1)} fusion(bf16[2,8,523,1024]{3,1,2,0:T(8,128)(2,1)} %get-tuple-element.170, s32[]{:T(128)} %get-tuple-element.162), kind=kLoop, calls=%fused_computation.2.clone.1 | loop fusion | bytes 33554436 | tf_op jit(solution)/shard_map/while/body/eval_jaxpr/dynamic_slice | solution.py:39
  174.8 0.8 constant_dynamic-slice_fusion.5
  175.6 27.2 %select_add_fusion.2 = f32[2,8,512,1024]{3,2,1,0:T(8,128)} fusion(f32[2,8,512,1024]{3,2,1,0:T(8,128)} %get-tuple-element.163, bf16[2,8,512,1024]{3,1,2,0:T(8,128)(2,1)} %constant_dynamic-slice_fusion.4, f32[1024]{0:T(1024)S(1)} %bitcast.50, pred[]{:T(512)S(6)} %compare.21), kind=kLoop, calls=%fused_computation.clone.1 | loop fusion | flops 33554432 | bytes 83890176 | tf_op jit(solution)/shard_map/while/body/eval_jaxpr/add | solution.py:41
  202.8 13.8 %constant_dynamic-slice_fusion.4 = bf16[2,8,512,1024]{3,1,2,0:T(8,128)(2,1)} fusion(bf16[2,8,523,1024]{3,1,2,0:T(8,128)(2,1)} %get-tuple-element.170, s32[]{:T(128)} %get-tuple-element.162), kind=kLoop, calls=%fused_computation.2.clone.1 | loop fusion | bytes 33554436 | tf_op jit(solution)/shard_map/while/body/eval_jaxpr/dynamic_slice | solution.py:39
  216.6 0.8 constant_dynamic-slice_fusion.5
  217.4 27.2 %select_add_fusion.2 = f32[2,8,512,1024]{3,2,1,0:T(8,128)} fusion(f32[2,8,512,1024]{3,2,1,0:T(8,128)} %get-tuple-element.163, bf16[2,8,512,1024]{3,1,2,0:T(8,128)(2,1)} %constant_dynamic-slice_fusion.4, f32[1024]{0:T(1024)S(1)} %bitcast.50, pred[]{:T(512)S(6)} %compare.21), kind=kLoop, calls=%fused_computation.clone.1 | loop fusion | flops 33554432 | bytes 83890176 | tf_op jit(solution)/shard_map/while/body/eval_jaxpr/add | solution.py:41
  244.6 13.8 %constant_dynamic-slice_fusion.4 = bf16[2,8,512,1024]{3,1,2,0:T(8,128)(2,1)} fusion(bf16[2,8,523,1024]{3,1,2,0:T(8,128)(2,1)} %get-tuple-element.170, s32[]{:T(128)} %get-tuple-element.162), kind=kLoop, calls=%fused_computation.2.clone.1 | loop fusion | bytes 33554436 | tf_op jit(solution)/shard_map/while/body/eval_jaxpr/dynamic_slice | solution.py:39
  258.4 0.8 constant_dynamic-slice_fusion.5
  259.2 27.2 %select_add_fusion.2 = f32[2,8,512,1024]{3,2,1,0:T(8,128)} fusion(f32[2,8,512,1024]{3,2,1,0:T(8,128)} %get-tuple-element.163, bf16[2,8,512,1024]{3,1,2,0:T(8,128)(2,1)} %constant_dynamic-slice_fusion.4, f32[1024]{0:T(1024)S(1)} %bitcast.50, pred[]{:T(512)S(6)} %compare.21), kind=kLoop, calls=%fused_computation.clone.1 | loop fusion | flops 33554432 | bytes 83890176 | tf_op jit(solution)/shard_map/while/body/eval_jaxpr/add | solution.py:41
  286.3 13.8 %constant_dynamic-slice_fusion.4 = bf16[2,8,512,1024]{3,1,2,0:T(8,128)(2,1)} fusion(bf16[2,8,523,1024]{3,1,2,0:T(8,128)(2,1)} %get-tuple-element.170, s32[]{:T(128)} %get-tuple-element.162), kind=kLoop, calls=%fused_computation.2.clone.1 | loop fusion | bytes 33554436 | tf_op jit(solution)/shard_map/while/body/eval_jaxpr/dynamic_slice | solution.py:39
  300.2 0.8 constant_dynamic-slice_fusion.5
  300.9 27.2 %select_add_fusion.2 = f32[2,8,512,1024]{3,2,1,0:T(8,128)} fusion(f32[2,8,512,1024]{3,2,1,0:T(8,128)} %get-tuple-element.163, bf16[2,8,512,1024]{3,1,2,0:T(8,128)(2,1)} %constant_dynamic-slice_fusion.4, f32[1024]{0:T(1024)S(1)} %bitcast.50, pred[]{:T(512)S(6)} %compare.21), kind=kLoop, calls=%fused_computation.clone.1 | loop fusion | flops 33554432 | bytes 83890176 | tf_op jit(solution)/shard_map/while/body/eval_jaxpr/add | solution.py:41
  328.1 13.8 %constant_dynamic-slice_fusion.4 = bf16[2,8,512,1024]{3,1,2,0:T(8,128)(2,1)} fusion(bf16[2,8,523,1024]{3,1,2,0:T(8,128)(2,1)} %get-tuple-element.170, s32[]{:T(128)} %get-tuple-element.162), kind=kLoop, calls=%fused_computation.2.clone.1 | loop fusion | bytes 33554436 | tf_op jit(solution)/shard_map/while/body/eval_jaxpr/dynamic_slice | solution.py:39
  342.0 0.8 constant_dynamic-slice_fusion.5
  342.7 27.2 %select_add_fusion.2 = f32[2,8,512,1024]{3,2,1,0:T(8,128)} fusion(f32[2,8,512,1024]{3,2,1,0:T(8,128)} %get-tuple-element.163, bf16[2,8,512,1024]{3,1,2,0:T(8,128)(2,1)} %constant_dynamic-slice_fusion.4, f32[1024]{0:T(1024)S(1)} %bitcast.50, pred[]{:T(512)S(6)} %compare.21), kind=kLoop, calls=%fused_computation.clone.1 | loop fusion | flops 33554432 | bytes 83890176 | tf_op jit(solution)/shard_map/while/body/eval_jaxpr/add | solution.py:41
  369.9 13.8 %constant_dynamic-slice_fusion.4 = bf16[2,8,512,1024]{3,1,2,0:T(8,128)(2,1)} fusion(bf16[2,8,523,1024]{3,1,2,0:T(8,128)(2,1)} %get-tuple-element.170, s32[]{:T(128)} %get-tuple-element.162), kind=kLoop, calls=%fused_computation.2.clone.1 | loop fusion | bytes 33554436 | tf_op jit(solution)/shard_map/while/body/eval_jaxpr/dynamic_slice | solution.py:39
  383.8 0.8 constant_dynamic-slice_fusion.5
  384.5 27.2 %select_add_fusion.2 = f32[2,8,512,1024]{3,2,1,0:T(8,128)} fusion(f32[2,8,512,1024]{3,2,1,0:T(8,128)} %get-tuple-element.163, bf16[2,8,512,1024]{3,1,2,0:T(8,128)(2,1)} %constant_dynamic-slice_fusion.4, f32[1024]{0:T(1024)S(1)} %bitcast.50, pred[]{:T(512)S(6)} %compare.21), kind=kLoop, calls=%fused_computation.clone.1 | loop fusion | flops 33554432 | bytes 83890176 | tf_op jit(solution)/shard_map/while/body/eval_jaxpr/add | solution.py:41
  411.7 13.8 %constant_dynamic-slice_fusion.4 = bf16[2,8,512,1024]{3,1,2,0:T(8,128)(2,1)} fusion(bf16[2,8,523,1024]{3,1,2,0:T(8,128)(2,1)} %get-tuple-element.170, s32[]{:T(128)} %get-tuple-element.162), kind=kLoop, calls=%fused_computation.2.clone.1 | loop fusion | bytes 33554436 | tf_op jit(solution)/shard_map/while/body/eval_jaxpr/dynamic_slice | solution.py:39
  425.5 0.8 constant_dynamic-slice_fusion.5
  426.3 27.2 %select_add_fusion.2 = f32[2,8,512,1024]{3,2,1,0:T(8,128)} fusion(f32[2,8,512,1024]{3,2,1,0:T(8,128)} %get-tuple-element.163, bf16[2,8,512,1024]{3,1,2,0:T(8,128)(2,1)} %constant_dynamic-slice_fusion.4, f32[1024]{0:T(1024)S(1)} %bitcast.50, pred[]{:T(512)S(6)} %compare.21), kind=kLoop, calls=%fused_computation.clone.1 | loop fusion | flops 33554432 | bytes 83890176 | tf_op jit(solution)/shard_map/while/body/eval_jaxpr/add | solution.py:41
  453.5 13.8 %constant_dynamic-slice_fusion.4 = bf16[2,8,512,1024]{3,1,2,0:T(8,128)(2,1)} fusion(bf16[2,8,523,1024]{3,1,2,0:T(8,128)(2,1)} %get-tuple-element.170, s32[]{:T(128)} %get-tuple-element.162), kind=kLoop, calls=%fused_computation.2.clone.1 | loop fusion | bytes 33554436 | tf_op jit(solution)/shard_map/while/body/eval_jaxpr/dynamic_slice | solution.py:39
  467.3 0.8 constant_dynamic-slice_fusion.5
  468.1 27.2 %select_add_fusion.2 = f32[2,8,512,1024]{3,2,1,0:T(8,128)} fusion(f32[2,8,512,1024]{3,2,1,0:T(8,128)} %get-tuple-element.163, bf16[2,8,512,1024]{3,1,2,0:T(8,128)(2,1)} %constant_dynamic-slice_fusion.4, f32[1024]{0:T(1024)S(1)} %bitcast.50, pred[]{:T(512)S(6)} %compare.21), kind=kLoop, calls=%fused_computation.clone.1 | loop fusion | flops 33554432 | bytes 83890176 | tf_op jit(solution)/shard_map/while/body/eval_jaxpr/add | solution.py:41
  495.3 0.0 copy-done.1
  495.3 0.0 copy-done.2
  495.3 2.5 fusion.19
  497.8 0.1 maximum_bitcast_fusion.3
  497.9 13.0 %bitcast_convert_fusion = bf16[128,2,8,512]{3,0,2,1:T(8,128)(2,1)S(1)} fusion(bf16[128,1,2,1024]{3,0,2,1:T(8,128)(2,1)S(1)} %get-tuple-element.127, bf16[128,1,2,1024]{3,0,2,1:T(8,128)(2,1)S(1)} %get-tuple-element.126, f32[2,8,512,1024]{3,2,1,0:T(8,128)} %get-tuple-element.84), kind=kOutput, calls=%fused_computation.11 | convolution fusion | flops 4306501632 | bytes 36700160 | tf_op jit(solution)/shard_map/dot_general | solution.py:56
  510.8 1.2 copy.23
  512.0 32.1 %all_to_all.20 = bf16[128,2,8,512]{3,2,1,0:T(8,128)(2,1)S(1)} all-to-all(bf16[128,2,8,512]{3,2,1,0:T(8,128)(2,1)S(1)} %copy.23), channel_id=1, replica_groups=mesh['chan'=8,'stn'=16] {'chan'}, dimensions={0} | all-to-all | bytes 4194304 | tf_op jit(solution)/shard_map/all_to_all | solution.py:59
  544.1 0.3 copy.41
  544.4 11.1 stack.64
  555.5 0.0 copy-start
  555.5 8.0 all-to-all-start.1
  563.4 0.0 copy-done
  563.4 0.1 broadcast_in_dim.7
  563.6 0.2 reshape.257
  563.7 0.1 dynamic_slice.17
  563.8 0.1 compare_select_fusion
  563.9 0.1 fusion.23
  564.1 1.5 maximum_bitcast_fusion
  565.6 615.4 %all-to-all-done.1 = bf16[16,16,2,64,512]{4,3,2,1,0:T(8,128)(2,1)} async-done(((bf16[16,16,2,64,512]{4,3,2,1,0:T(8,128)(2,1)}), bf16[16,16,2,64,512]{4,3,2,1,0:T(8,128)(2,1)}, u32[]{:S(2)}, u32[]{:S(2)}) %all-to-all-start.1) | async-done | bytes 33554464 | tf_op jit(solution)/shard_map/all_to_all | solution.py:65
  1181.0 22.9 %copy.25 = bf16[16,2,16,64,512]{4,3,2,1,0:T(8,128)(2,1)} copy(bf16[16,2,16,64,512]{4,3,1,0,2:T(8,128)(2,1)} %bitcast.11) | data formatting | bytes 67108864 | tf_op jit(solution)/shard_map/reshape | solution.py:64
  1203.9 18.7 %bitcast_multiply_fusion = f32[64,2,16,1024]{3,0,1,2:T(8,128)} fusion(f32[64,1024]{1,0:T(8,128)S(1)} %compare_select_fusion, bf16[16,2,1024,512,1]{3,2,1,4,0:T(8,128)(2,1)} %bitcast.45, bf16[1,16,2,64,512]{4,3,2,0,1:T(8,128)(2,1)} %maximum_bitcast_fusion, bf16[1,16,2,64,512]{4,3,2,0,1:T(8,128)(2,1)S(1)} %bitcast.48), kind=kOutput, calls=%fused_computation.6 | convolution fusion | flops 4305453056 | bytes 46399488 | tf_op jit(solution)/shard_map/osrit,srjt->iosj/dot_general | solution.py:50
  1222.7 11.6 copy.26
  (2 shorter events, 0.0 us)
Async XLA Ops:
  1.8 493.5 %copy-start.1 = (f32[128]{0:T(128)S(1)}, f32[128]{0:T(128)}, u32[]{:S(2)}) copy-start(f32[128]{0:T(128)} %compare_select_fusion.1) | copy-start | bytes 1540
  1.8 493.5 %copy-start.2 = (s32[128]{0:T(128)S(1)}, s32[128]{0:T(128)}, u32[]{:S(2)}) copy-start(s32[128]{0:T(128)} %fusion.20) | copy-start | bytes 1540
  555.5 8.0 copy-start
  555.5 625.6 %all-to-all-start.1 = ((bf16[16,16,2,64,512]{4,3,2,1,0:T(8,128)(2,1)}), bf16[16,16,2,64,512]{4,3,2,1,0:T(8,128)(2,1)}, u32[]{:S(2)}, u32[]{:S(2)}) async-start(bf16[16,16,2,64,512]{4,3,2,1,0:T(8,128)(2,1)} %stack.64), calls=%async_computation.1 | async-start | bytes 67108864 | tf_op jit(solution)/shard_map/all_to_all | solution.py:65
